TPU v7x, 32 devices: a whole 2x2x4 slice. The times are simulated.
32 devices in a mesh: dp: 4 (over y, x), mp: 8 (over z, core).
Axes of the slice: x: 2, y: 2, z: 4, core: 2. Of those that a mesh axis runs over, the one named last changes fastest.
Arguments:
- activations: bfloat16 [4096, 2048], P('dp', 'mp'), may hold values from -6 to 6
- out_grad: bfloat16 [4096, 8192], P('dp'), may hold values from -0.8984375 to 0.8984375
- old_weight: bfloat16 [8, 256, 8192], P('mp', 'dp'), may hold values from -0.125 to 0.125
- old_first: float32 [8, 256, 8192], P('mp', 'dp'), may hold values from -6 to 6
- old_second: float32 [8, 256, 8192], P('mp', 'dp'), may hold values from 0.25 to 4
- step: int32 [1], replicated, may hold values from 1 to 31
- next_input: bfloat16 [4096, 2048], P('dp', 'mp'), may hold values from -6 to 6
Outputs:
- new_weight: bfloat16 [8, 344, 8192], P('mp', 'dp')
- new_first: float32 [8, 344, 8192], P('mp', 'dp')
- new_second: float32 [8, 344, 8192], P('mp', 'dp')
- output: bfloat16 [4096, 8192], P('dp', 'mp')
Inputs may be any that keep to these rules, and one draw needn't show every extreme that they name: `step`: the number of Adam steps taken, this one included.
All inputs are finite; a program needn't handle non-finite values.
Results may differ from a plain program's by a relative error of at most 0.0049.
Values may be sent and summed in bfloat16 or wider, within the bound.
A program may use at most 192 MiB of HBM per device.

v0:
```python
import jax
import jax.numpy as jnp
from jax import lax
from jax.sharding import PartitionSpec as P


def partner(i, k, n):
    return i ^ k if n & n - 1 == 0 else (i + k) % n


def exchange(block, axis, k):
    n = lax.axis_size(axis)
    return lax.ppermute(block, axis, [(i, partner(i, k, n)) for i in range(n)])


def target(k, n, axis):
    me = lax.axis_index(axis)
    return me ^ k if n & n - 1 == 0 else lax.rem(me + k, n)


def to_front(block, axis):
    n = lax.axis_size(axis)
    return lax.ppermute(block, axis, [(i, i - 1) for i in range(1, n)])


def body(activations, out_grad, old_weight, old_first, old_second, step, next_input):
    owners = lax.axis_size("dp")
    owner = lax.axis_index("dp")
    old_rows = old_weight.shape[1]
    width = old_weight.shape[2]
    held_rows = old_rows * owners
    shard_rows = (held_rows + owners - 2) // (owners - 1)
    input_all = lax.all_gather(next_input, "mp", axis=1, tiled=True)
    part = lax.dot_general(
        activations, out_grad, (((0,), (0,)), ((), ())), preferred_element_type=jnp.float32
    ).astype(jnp.bfloat16)
    part = part.reshape(owners, old_rows, width)
    grad = lax.dynamic_index_in_dim(part, owner, 0, keepdims=False).astype(jnp.float32)
    for k in range(1, owners):
        away = lax.dynamic_index_in_dim(part, target(k, owners, "dp"), 0, keepdims=False)
        grad = grad + exchange(away, "dp", k).astype(jnp.float32)
    step_float = step[0].astype(jnp.float32)
    first_fix = 1.0 - jnp.power(jnp.float32(0.9), step_float)
    second_fix = 1.0 - jnp.power(jnp.float32(0.95), step_float)
    new_first = 0.9 * old_first[0] + 0.1 * grad
    new_second = 0.95 * old_second[0] + 0.05 * grad * grad
    update = new_first / first_fix / (jnp.sqrt(new_second / second_fix) + 1e-08)
    new_weight = (old_weight[0].astype(jnp.float32) - 0.01 * update).astype(jnp.bfloat16)
    weight_part = lax.all_to_all(new_weight, "mp", split_axis=1, concat_axis=0, tiled=True)
    heads = lax.axis_size("mp")
    weight_part = weight_part.reshape(heads, old_rows, -1)
    weight_cols = lax.all_gather(weight_part, "dp", axis=1, tiled=True)
    weight_cols = weight_cols.reshape(heads * held_rows, -1)
    begin = owner * (shard_rows - old_rows)

    def mine(block):
        behind = to_front(block.astype(jnp.bfloat16), "dp").astype(block.dtype)
        rows = jnp.concatenate([block, behind, jnp.zeros((shard_rows, width), block.dtype)], 0)
        return lax.dynamic_slice_in_dim(rows, begin, shard_rows, 0)[None]

    outs = (mine(new_weight), mine(new_first), mine(new_second))
    output = jnp.dot(input_all, weight_cols, preferred_element_type=jnp.float32).astype(
        jnp.bfloat16
    )
    return (*outs, output)


def solution(mesh):
    return jax.shard_map(
        body,
        mesh=mesh,
        in_specs=(
            P("dp", "mp"),
            P("dp", None),
            P("mp", "dp", None),
            P("mp", "dp", None),
            P("mp", "dp", None),
            P(),
            P("dp", "mp"),
        ),
        out_specs=(P("mp", "dp", None), P("mp", "dp", None), P("mp", "dp", None), P("dp", "mp")),
        check_vma=False,
    )
```

profile of v0, /device:TPU:0, one launch (start us, length us, event | category | flops | bytes accessed | tf_op | source)
XLA Modules:
  0.0 292.9 jit_solution(17170010049314651664)
XLA Ops:
  8.2 10.7 %convolution_convert_fusion = bf16[256,8192]{1,0:T(8,128)(2,1)S(1)} fusion(bf16[1024,256]{1,0:T(8,128)(2,1)S(1)} %copy-done, bf16[1024,8192]{1,0:T(8,128)(2,1)} %param.8), kind=kOutput, calls=%fused_computation | convolution fusion | flops 4297064448 | bytes 21495808 | tf_op jit(solution)/shard_map/dot_general | solution.py:34
  19.0 1.8 dynamic-slice_bitcast_fusion.2
  21.9 2.9 %collective-permute-start = (bf16[64,8192]{1,0:T(8,128)(2,1)}, bf16[64,8192]{1,0:T(8,128)(2,1)S(1)}, u32[]{:S(2)}, u32[]{:S(2)}) collective-permute-start(bf16[64,8192]{1,0:T(8,128)(2,1)} %get-tuple-element.26), channel_id=1, source_target_pairs={{0,8},{8,0},{16,24},{24,16},{1,9},{9,1},{17,25},{25,17},{2,10},{10... | collective-permute-start | bytes 3145736 | tf_op jit(solution)/shard_map/ppermute | solution.py:13
  24.8 1.5 collective-permute-start.1
  27.1 21.9 %collective-permute-done = bf16[64,8192]{1,0:T(8,128)(2,1)S(1)} collective-permute-done((bf16[64,8192]{1,0:T(8,128)(2,1)}, bf16[64,8192]{1,0:T(8,128)(2,1)S(1)}, u32[]{:S(2)}, u32[]{:S(2)}) %collective-permute-start) | collective-permute-done | bytes 1048608 | tf_op jit(solution)/shard_map/ppermute | solution.py:13
  49.0 23.1 %collective-permute-done.1 = bf16[64,8192]{1,0:T(8,128)(2,1)S(1)} collective-permute-done((bf16[64,8192]{1,0:T(8,128)(2,1)}, bf16[64,8192]{1,0:T(8,128)(2,1)S(1)}, u32[]{:S(2)}, u32[]{:S(2)}) %collective-permute-start.1) | collective-permute-done | bytes 1048608 | tf_op jit(solution)/shard_map/ppermute | solution.py:13
  73.1 5.9 %fusion.11 = (bf16[64,8192]{1,0:T(8,128)(2,1)}, f32[64,8192]{1,0:T(8,128)S(1)}, bf16[64,8192]{1,0:T(8,128)(2,1)}, f32[64,8192]{1,0:T(8,128)S(1)}) fusion(bf16[64,8192]{1,0:T(8,128)(2,1)} %collective-permute-done.2, bf16[64,8192]{1,0:T(8,128)(2,1)} %copy-done.8, bf16[64,8192]{1,0:T(8,128)(2,1)} %copy-done.7, bf16[4,64,8192]{2,1,0:T(8,128)(2,1)} %bitcast.42, ...), kind=kLoop, calls=%fused_computation.29 | loop fusion | flops 8388608 | bytes 14680068 | tf_op jit(solution)/shard_map/convert_element_type | solution.py:57
  80.4 31.3 %all_to_all.16 = bf16[64,8,1024]{2,0,1:T(8,128)(2,1)S(1)} all-to-all(bf16[64,8,1024]{2,0,1:T(8,128)(2,1)S(1)} %bitcast.46), channel_id=1, replica_groups=mesh['dp'=4,'mp'=8] {'mp'}, dimensions={1} | all-to-all | bytes 2097152 | tf_op jit(solution)/shard_map/all_to_all | solution.py:49
  111.7 1.5 copy.16
  116.8 1.5 collective-permute-start.3
  118.2 35.3 %collective-permute-done.4 = bf16[64,8192]{1,0:T(8,128)(2,1)} collective-permute-done((bf16[64,8192]{1,0:T(8,128)(2,1)}, bf16[64,8192]{1,0:T(8,128)(2,1)}, u32[]{:S(2)}, u32[]{:S(2)}) %collective-permute-start.4) | collective-permute-done | bytes 1048608 | tf_op jit(solution)/shard_map/ppermute | solution.py:23
  153.5 1.4 convert_element_type.60
  154.9 21.1 %collective-permute-done.5 = bf16[64,8192]{1,0:T(8,128)(2,1)} collective-permute-done((bf16[64,8192]{1,0:T(8,128)(2,1)}, bf16[64,8192]{1,0:T(8,128)(2,1)}, u32[]{:S(2)}, u32[]{:S(2)}) %collective-permute-start.5) | collective-permute-done | bytes 1048608 | tf_op jit(solution)/shard_map/ppermute | solution.py:23
  176.0 1.4 convert_element_type.62
  177.4 4.0 %fusion.1 = (f32[86,8192]{1,0:T(8,128)}, f32[86,8192]{1,0:T(8,128)}) fusion(s32[]{:T(128)S(6)} %select_n.22, f32[64,8192]{1,0:T(8,128)S(1)} %get-tuple-element.21, f32[64,8192]{1,0:T(8,128)S(1)} %convert_element_type.62, f32[86]{0:T(128)S(1)} %pad_dynamic-slice_fusion.6, f32[64,8192]{1,0:T(8,128)S(1)} %convert_element_type.60, f32[64,8192]{1,0:T(8,128)S(1)} %copy-done.3), kind=kLoop, calls=%fused_computation.9 | loop fusion | flops 2818048 | bytes 14025052 | tf_op jit(solution)/shard_map/concatenate | solution.py:58
  181.3 6.7 %broadcast_in_dim.14 = f32[1,86,8192]{2,0,1:T(1,128)} reshape(f32[86,8192]{1,0:T(8,128)} %get-tuple-element.30) | data formatting | bytes 5636096 | tf_op jit(solution)/shard_map/broadcast_in_dim | solution.py:59
  188.0 4.7 %broadcast_in_dim.15 = f32[1,86,8192]{2,0,1:T(1,128)} reshape(f32[86,8192]{1,0:T(8,128)S(1)} %copy-done.5) | data formatting | bytes 5636096 | tf_op jit(solution)/shard_map/broadcast_in_dim | solution.py:59
  192.8 4.1 %collective-permute-done.3 = bf16[64,8192]{1,0:T(8,128)(2,1)} collective-permute-done((bf16[64,8192]{1,0:T(8,128)(2,1)}, bf16[64,8192]{1,0:T(8,128)(2,1)}, u32[]{:S(2)}, u32[]{:S(2)}) %collective-permute-start.3) | collective-permute-done | bytes 1048608 | tf_op jit(solution)/shard_map/ppermute | solution.py:23
  196.9 3.4 %fusion.10 = bf16[1,86,8192]{2,1,0:T(8,128)(2,1)} fusion(s32[]{:T(128)S(6)} %select_n.22, bf16[64,8192]{1,0:T(8,128)(2,1)} %copy-done.6, bf16[64,8192]{1,0:T(8,128)(2,1)} %collective-permute-done.3, bf16[86]{0:T(256)(128)(2,1)S(1)} %pad_dynamic-slice_fusion.7), kind=kLoop, calls=%fused_computation.22 | loop fusion | flops 4227072 | bytes 3506352 | tf_op jit(solution)/shard_map/broadcast_in_dim | solution.py:59
  200.3 25.5 %all-gather.3.cloned.1.call-done = bf16[8,256,1024]{2,0,1:T(8,128)(2,1)} async-done(((bf16[8,64,1024]{2,0,1:T(8,128)(2,1)}), bf16[8,256,1024]{2,0,1:T(8,128)(2,1)}) %all-gather.3.cloned.1.call-update) | async-done | bytes 4194320 | tf_op jit(solution)/shard_map/all_gather | solution.py:52
  225.8 6.5 %copy.17 = bf16[8,256,1024]{2,1,0:T(8,128)(2,1)} copy(bf16[8,256,1024]{2,0,1:T(8,128)(2,1)} %all-gather.3.cloned.1.call-done) | data formatting | bytes 8388608 | tf_op jit(solution)/shard_map/all_gather | solution.py:52
  232.3 42.9 %all-gather.5.cloned.1.call-done = bf16[1024,2048]{1,0:T(8,128)(2,1)} async-done(((bf16[1024,256]{1,0:T(8,128)(2,1)}), bf16[1024,2048]{1,0:T(8,128)(2,1)}) %all-gather.5.cloned.1.call-update) | async-done | bytes 4194320 | tf_op jit(solution)/shard_map/all_gather | solution.py:33
  275.2 8.3 %convert_bitcast_fusion = bf16[1024,1024]{0,1:T(8,128)(2,1)S(1)} fusion(bf16[2048,1024]{1,0:T(8,128)(2,1)} %bitcast.44, bf16[1024,2048]{1,0:T(8,128)(2,1)} %all-gather.5.cloned.1.call-done), kind=kOutput, calls=%fused_computation.19 | convolution fusion | flops 4296015872 | bytes 10485760 | tf_op jit(solution)/shard_map/dot_general | solution.py:62
  283.5 2.6 copy.18
  (34 shorter events, 8.1 us)
Async XLA Ops:
  7.2 1.1 copy-start
  7.2 218.6 %all-gather.3.cloned.1.call-start = ((), (), s32[]{:S(2)}) async-start(), calls=%async_computation.1 | async-start | bytes 5242880 | tf_op jit(solution)/shard_map/all_gather | solution.py:52
  19.0 2.9 %copy-start.4 = (bf16[256,8192]{1,0:T(8,128)(2,1)}, bf16[256,8192]{1,0:T(8,128)(2,1)S(1)}, u32[]{:S(2)}) copy-start(bf16[256,8192]{1,0:T(8,128)(2,1)S(1)} %convolution_convert_fusion) | copy-start | bytes 12582916
  21.9 27.1 %collective-permute-start = (bf16[64,8192]{1,0:T(8,128)(2,1)}, bf16[64,8192]{1,0:T(8,128)(2,1)S(1)}, u32[]{:S(2)}, u32[]{:S(2)}) collective-permute-start(bf16[64,8192]{1,0:T(8,128)(2,1)} %get-tuple-element.26), channel_id=1, source_target_pairs={{0,8},{8,0},{16,24},{24,16},{1,9},{9,1},{17,25},{25,17},{2,10},{10... | collective-permute-start | bytes 3145736 | tf_op jit(solution)/shard_map/ppermute | solution.py:13
  24.8 47.3 %collective-permute-start.1 = (bf16[64,8192]{1,0:T(8,128)(2,1)}, bf16[64,8192]{1,0:T(8,128)(2,1)S(1)}, u32[]{:S(2)}, u32[]{:S(2)}) collective-permute-start(bf16[64,8192]{1,0:T(8,128)(2,1)} %get-tuple-element.28), channel_id=1, source_target_pairs={{0,16},{8,24},{16,0},{24,8},{1,17},{9,25},{17,1},{25,9},{2,18},{10... | collective-permute-start | bytes 3145736 | tf_op jit(solution)/shard_map/ppermute | solution.py:13
  26.4 46.8 %collective-permute-start.2 = (bf16[64,8192]{1,0:T(8,128)(2,1)}, bf16[64,8192]{1,0:T(8,128)(2,1)}, u32[]{:S(2)}, u32[]{:S(2)}) collective-permute-start(bf16[64,8192]{1,0:T(8,128)(2,1)} %get-tuple-element.27), channel_id=1, source_target_pairs={{0,24},{8,16},{16,8},{24,0},{1,25},{9,17},{17,9},{25,1},{2,26},{10... | collective-permute-start | bytes 3145736 | tf_op jit(solution)/shard_map/ppermute | solution.py:13
  27.1 51.9 %copy-start.9 = (bf16[1,64,8192]{2,1,0:T(8,128)(2,1)S(1)}, bf16[1,64,8192]{2,1,0:T(8,128)(2,1)}, u32[]{:S(2)}) copy-start(bf16[1,64,8192]{2,1,0:T(8,128)(2,1)} %param.9) | copy-start | bytes 3145732
  49.0 23.1 %copy-start.7 = (bf16[64,8192]{1,0:T(8,128)(2,1)}, bf16[64,8192]{1,0:T(8,128)(2,1)S(1)}, u32[]{:S(2)}) copy-start(bf16[64,8192]{1,0:T(8,128)(2,1)S(1)} %collective-permute-done) | copy-start | bytes 3145732
  72.2 1.0 copy-start.8
  79.0 1.3 copy-start.2
  80.3 31.4 %copy-start.6 = (bf16[64,8192]{1,0:T(8,128)(2,1)}, bf16[64,8192]{1,0:T(8,128)(2,1)S(1)}, u32[]{:S(2)}) copy-start(bf16[64,8192]{1,0:T(8,128)(2,1)S(1)} %fusion.7) | copy-start | bytes 3145732
  113.2 162.0 %all-gather.5.cloned.1.call-start = ((), (), s32[]{:S(2)}) async-start(), calls=%async_computation.2 | async-start | bytes 4718592 | tf_op jit(solution)/shard_map/all_gather | solution.py:33
  114.0 39.5 %collective-permute-start.4 = (bf16[64,8192]{1,0:T(8,128)(2,1)}, bf16[64,8192]{1,0:T(8,128)(2,1)}, u32[]{:S(2)}, u32[]{:S(2)}) collective-permute-start(bf16[64,8192]{1,0:T(8,128)(2,1)} %get-tuple-element.24), channel_id=1, source_target_pairs={{8,0},{16,8},{24,16},{9,1},{17,9},{25,17},{10,2},{18,10},{26,18},{... | collective-permute-start | bytes 3145736 | tf_op jit(solution)/shard_map/ppermute | solution.py:23
  115.3 60.7 %collective-permute-start.5 = (bf16[64,8192]{1,0:T(8,128)(2,1)}, bf16[64,8192]{1,0:T(8,128)(2,1)}, u32[]{:S(2)}, u32[]{:S(2)}) collective-permute-start(bf16[64,8192]{1,0:T(8,128)(2,1)} %get-tuple-element.20), channel_id=1, source_target_pairs={{8,0},{16,8},{24,16},{9,1},{17,9},{25,17},{10,2},{18,10},{26,18},{... | collective-permute-start | bytes 3145736 | tf_op jit(solution)/shard_map/ppermute | solution.py:23
  116.8 80.1 %collective-permute-start.3 = (bf16[64,8192]{1,0:T(8,128)(2,1)}, bf16[64,8192]{1,0:T(8,128)(2,1)}, u32[]{:S(2)}, u32[]{:S(2)}) collective-permute-start(bf16[64,8192]{1,0:T(8,128)(2,1)} %copy-done.6), channel_id=1, source_target_pairs={{8,0},{16,8},{24,16},{9,1},{17,9},{25,17},{10,2},{18,10},{26,18},{... | collective-permute-start | bytes 3145736 | tf_op jit(solution)/shard_map/ppermute | solution.py:23
  154.9 22.5 %copy-start.3 = (f32[64,8192]{1,0:T(8,128)S(1)}, f32[64,8192]{1,0:T(8,128)}, u32[]{:S(2)}) copy-start(f32[64,8192]{1,0:T(8,128)} %copy-done.2) | copy-start | bytes 6291460
  181.3 6.7 %copy-start.5 = (f32[86,8192]{1,0:T(8,128)S(1)}, f32[86,8192]{1,0:T(8,128)}, u32[]{:S(2)}) copy-start(f32[86,8192]{1,0:T(8,128)} %get-tuple-element.29) | copy-start | bytes 8454148
  275.2 10.9 %copy-start.1 = (bf16[1024,256]{1,0:T(8,128)(2,1)S(1)}, bf16[1024,256]{1,0:T(8,128)(2,1)}, u32[]{:S(2)}) copy-start(bf16[1024,256]{1,0:T(8,128)(2,1)} %param.7) | copy-start | bytes 1572868
Sparse Core Ops, SparseCore 0:
  113.3 112.3 all-gather.2
  227.4 47.7 all-gather.4
where the time goes:
time: 293 us
  waiting for transfers between devices  175 us (60%)
  blocking collectives  31.3 us (11%)
  local copies, waits for them, and re-layouts  27.4 us (9%)
  matrix products  19 us (6%)
  other arithmetic  17 us (6%)
  between operations  14.9 us (5%)
  starting transfers between devices  8.58 us (3%)
    ppermute x3, waiting for transfers between devices, to_front(): return lax.ppermute(block, axis, [(i, i - 1) for i in range(1, n)])  60.5 us
    ppermute x3, waiting for transfers between devices, exchange(): return lax.ppermute(block, axis, [(i, partner(i, k, n)) for i in range(n)])  45 us
    all_gather x1, waiting for transfers between devices, body(): input_all = lax.all_gather(next_input, 'mp', axis=1, tiled=True)  42.9 us
    all_to_all x1, blocking collectives, body(): lax.all_to_all(new_weight, 'mp', split_axis=1, concat_axis=0, tiled=True)  31.3 us
    all_gather x1, waiting for transfers between devices, body(): weight_cols = lax.all_gather(weight_part, 'dp', axis=1, tiled=True)  25.5 us
    broadcast_in_dim x2, local copies, waits for them, and re-layouts, mine(): return lax.dynamic_slice_in_dim(rows, begin, shard_rows, 0)[None]  11.4 us
    dot_general x1, matrix products, body(): lax.dot_general(activations, out_grad, (((0,), (0,)), ((), ())), preferre...  10.7 us
    convert_element_type x3, other arithmetic, mine(): behind = to_front(block.astype(jnp.bfloat16), 'dp').astype(block.dtype)  8.57 us
  transfers between devices with their start and end apart: 8, of which 7 were waited for; matrix products, arithmetic and copies ran while one was open for 10% of the time, Pallas kernels for 0%

commit v1 on v0

--- a/solution.py
+++ b/solution.py
@@ -2,6 +2,18 @@
 import jax.numpy as jnp
 from jax import lax
 from jax.sharding import PartitionSpec as P
+
+
+def in_blocks(x, dim, count):
+    lengths = x.shape
+    blocks = x.reshape(*lengths[:dim], count, lengths[dim] // count, *lengths[dim + 1 :])
+    return jnp.moveaxis(blocks, dim, 0)
+
+
+def laid_out(blocks, dim):
+    blocks = jnp.moveaxis(blocks, 0, dim)
+    dims = blocks.shape
+    return blocks.reshape(*dims[:dim], dims[dim] * dims[dim + 1], *dims[dim + 2 :])
 
 
 def partner(i, k, n):
@@ -46,7 +58,16 @@
     new_second = 0.95 * old_second[0] + 0.05 * grad * grad
     update = new_first / first_fix / (jnp.sqrt(new_second / second_fix) + 1e-08)
     new_weight = (old_weight[0].astype(jnp.float32) - 0.01 * update).astype(jnp.bfloat16)
-    weight_part = lax.all_to_all(new_weight, "mp", split_axis=1, concat_axis=0, tiled=True)
+    peers, here = (lax.axis_size("mp"), lax.axis_index("mp"))
+    blocks = in_blocks(new_weight, 1, peers)
+    outs_2 = [blocks[here]]
+    for hop in range(1, peers):
+        sent = blocks[(here + hop) % peers]
+        outs_2.append(
+            lax.ppermute(sent, "mp", [(i_2, (i_2 + hop) % peers) for i_2 in range(peers)])
+        )
+    blocks = jnp.stack(outs_2)[(here - jnp.arange(peers)) % peers]
+    weight_part = laid_out(blocks, 0)
     heads = lax.axis_size("mp")
     weight_part = weight_part.reshape(heads, old_rows, -1)
     weight_cols = lax.all_gather(weight_part, "dp", axis=1, tiled=True)

time: 293 us -> 248 us (0.85)
  blocking collectives: 31.3 us -> 0 us
  waiting for transfers between devices: 175 us -> 146 us
  starting transfers between devices: 8.58 us -> 18.3 us
  local copies, waits for them, and re-layouts: 27.4 us -> 30.7 us
    all_gather x1, waiting for transfers between devices: 42.9 us -> 0.01 us  [body(): input_all = lax.all_gather(next_input, 'mp', axis=1, tiled=True)]
    all_to_all x1 -> x0, blocking collectives: 31.3 us -> none  [body(): lax.all_to_all(new_weight, 'mp', split_axis=1, concat_axis=0, tiled=True)]
    ppermute x0 -> x7, starting transfers between devices: none -> 9.81 us  [body(): lax.ppermute(sent, 'mp', [(i_2, (i_2 + hop) % peers) for i_2 in range(pee...]
    all_gather x1, waiting for transfers between devices: 25.5 us -> 33.4 us  [body(): weight_cols = lax.all_gather(weight_part, 'dp', axis=1, tiled=True)]
    ppermute x0 -> x7, waiting for transfers between devices: none -> 6.67 us  [body(): lax.ppermute(sent, 'mp', [(i_2, (i_2 + hop) % peers) for i_2 in range(pee...]
    all_gather x1 -> x0, local copies, waits for them, and re-layouts: 6.49 us -> none  [body(): weight_cols = lax.all_gather(weight_part, 'dp', axis=1, tiled=True)]
    unnamed x21 -> x34, local copies, waits for them, and re-layouts: 5.95 us -> 9.64 us
    another operation x1 -> x3, local copies, waits for them, and re-layouts: 0.01 us -> 2.95 us
  transfers between devices with their start and end apart: 8 -> 15, of which waited for: 7 -> 7; matrix products, arithmetic and copies ran while one was open for 10% -> 23% of each run, Pallas kernels for 0% -> 0%
where the time goes in v1:
time: 248 us
  waiting for transfers between devices  146 us (59%)
  local copies, waits for them, and re-layouts  30.7 us (12%)
  matrix products  20.2 us (8%)
  starting transfers between devices  18.3 us (7%)
  other arithmetic  17 us (7%)
  between operations  15 us (6%)
    ppermute x3, waiting for transfers between devices, to_front(): return lax.ppermute(block, axis, [(i, i - 1) for i in range(1, n)])  61 us
    ppermute x3, waiting for transfers between devices, exchange(): return lax.ppermute(block, axis, [(i, partner(i, k, n)) for i in range(n)])  44.5 us
    all_gather x1, waiting for transfers between devices, body(): weight_cols = lax.all_gather(weight_part, 'dp', axis=1, tiled=True)  33.4 us
    dot_general x1, matrix products, body(): lax.dot_general(activations, out_grad, (((0,), (0,)), ((), ())), preferre...  12.1 us
    broadcast_in_dim x2, local copies, waits for them, and re-layouts, mine(): return lax.dynamic_slice_in_dim(rows, begin, shard_rows, 0)[None]  11.4 us
    ppermute x7, starting transfers between devices, body(): lax.ppermute(sent, 'mp', [(i_2, (i_2 + hop) % peers) for i_2 in range(pee...  9.81 us
    unnamed x34, local copies, waits for them, and re-layouts  9.64 us
    convert_element_type x3, other arithmetic, mine(): behind = to_front(block.astype(jnp.bfloat16), 'dp').astype(block.dtype)  8.57 us
  transfers between devices with their start and end apart: 15, of which 7 were waited for; matrix products, arithmetic and copies ran while one was open for 23% of the time, Pallas kernels for 0%

profile of v1, /device:TPU:0, one launch (start us, length us, event | category | flops | bytes accessed | tf_op | source)
XLA Modules:
  0.0 247.5 jit_solution(18103829863174968420)
XLA Ops:
  8.2 12.1 %convolution_convert_fusion = bf16[256,8192]{1,0:T(8,128)(2,1)} fusion(bf16[1024,256]{1,0:T(8,128)(2,1)S(1)} %copy-done, bf16[1024,8192]{1,0:T(8,128)(2,1)} %param.8), kind=kOutput, calls=%fused_computation.1 | convolution fusion | flops 4297064448 | bytes 21495808 | tf_op jit(solution)/shard_map/dot_general | solution.py:46
  20.3 3.7 %dynamic-slice_bitcast_fusion.2 = (bf16[64,8192]{1,0:T(8,128)(2,1)}, bf16[64,8192]{1,0:T(8,128)(2,1)}, bf16[64,8192]{1,0:T(8,128)(2,1)}) fusion(bf16[4,64,8192]{2,1,0:T(8,128)(2,1)} %bitcast.77, s32[]{:T(128)S(6)} %select_n.97, s32[]{:T(128)S(6)} %select_n.99, s32[]{:T(128)S(6)} %select_n.98), kind=kLoop, calls=%fused_computation.26 | loop fusion | bytes 6291468 | tf_op jit(solution)/shard_map/jit(dynamic_index_in_dim)/squeeze | solution.py:52
  24.1 3.8 %collective-permute-start.2 = (bf16[64,8192]{1,0:T(8,128)(2,1)}, bf16[64,8192]{1,0:T(8,128)(2,1)S(1)}, u32[]{:S(2)}, u32[]{:S(2)}) collective-permute-start(bf16[64,8192]{1,0:T(8,128)(2,1)} %get-tuple-element.23), channel_id=1, source_target_pairs={{0,24},{8,16},{16,8},{24,0},{1,25},{9,17},{17,9},{25,1},{2,26},{10... | collective-permute-start | bytes 3145736 | tf_op jit(solution)/shard_map/ppermute | solution.py:25
  29.3 22.9 %collective-permute-done.2 = bf16[64,8192]{1,0:T(8,128)(2,1)S(1)} collective-permute-done((bf16[64,8192]{1,0:T(8,128)(2,1)}, bf16[64,8192]{1,0:T(8,128)(2,1)S(1)}, u32[]{:S(2)}, u32[]{:S(2)}) %collective-permute-start.2) | collective-permute-done | bytes 1048608 | tf_op jit(solution)/shard_map/ppermute | solution.py:25
  52.1 21.6 %collective-permute-done.1 = bf16[64,8192]{1,0:T(8,128)(2,1)S(1)} collective-permute-done((bf16[64,8192]{1,0:T(8,128)(2,1)}, bf16[64,8192]{1,0:T(8,128)(2,1)S(1)}, u32[]{:S(2)}, u32[]{:S(2)}) %collective-permute-start.1) | collective-permute-done | bytes 1048608 | tf_op jit(solution)/shard_map/ppermute | solution.py:25
  74.7 5.9 %fusion.13 = (bf16[64,8192]{1,0:T(8,128)(2,1)}, f32[64,8192]{1,0:T(8,128)S(1)}, bf16[64,8192]{1,0:T(8,128)(2,1)}, f32[64,8192]{1,0:T(8,128)S(1)}) fusion(bf16[64,8192]{1,0:T(8,128)(2,1)} %copy-done.6, bf16[64,8192]{1,0:T(8,128)(2,1)} %copy-done.7, bf16[64,8192]{1,0:T(8,128)(2,1)} %collective-permute-done, bf16[4,64,8192]{2,1,0:T(8,128)(2,1)} %bitcast.78, ...), kind=kLoop, calls=%fused_computation.59 | loop fusion | flops 8388608 | bytes 14680068 | tf_op jit(solution)/shard_map/convert_element_type | solution.py:78
  82.5 2.3 constant_dynamic-slice_fusion
  85.0 1.8 collective-permute-start.7
  86.9 2.5 %collective-permute-start.8 = (bf16[64,1024]{1,0:T(8,128)(2,1)S(1)}, bf16[64,1024]{1,0:T(8,128)(2,1)S(1)}, u32[]{:S(2)}, u32[]{:S(2)}) collective-permute-start(bf16[64,1024]{1,0:T(8,128)(2,1)S(1)} %bitcast.85), channel_id=1, source_target_pairs={{0,3},{1,4},{2,5},{3,6},{4,7},{5,0},{6,1},{7,2},{8,11},{9,12},{10,... | collective-permute-start | bytes 393224 | tf_op jit(solution)/shard_map/ppermute | solution.py:67
  97.0 6.7 %collective-permute-done.8 = bf16[64,1024]{1,0:T(8,128)(2,1)S(1)} collective-permute-done((bf16[64,1024]{1,0:T(8,128)(2,1)S(1)}, bf16[64,1024]{1,0:T(8,128)(2,1)S(1)}, u32[]{:S(2)}, u32[]{:S(2)}) %collective-permute-start.8) | collective-permute-done | bytes 131104 | tf_op jit(solution)/shard_map/ppermute | solution.py:67
  106.9 2.8 %gather_fusion = bf16[8,64,1024]{2,1,0:T(8,128)(2,1)} fusion(bf16[8,64,1024]{2,1,0:T(8,128)(2,1)} %bitcast_dynamic-update-slice_fusion.1, s32[1024]{0:T(1024)S(1)} %pad_clamp_fusion), kind=kCustom, calls=%fused_computation | custom fusion | bytes 2097184 | tf_op jit(solution)/shard_map/gather | solution.py:69
  112.6 1.5 collective-permute-start.3
  114.0 33.9 %collective-permute-done.5 = bf16[64,8192]{1,0:T(8,128)(2,1)} collective-permute-done((bf16[64,8192]{1,0:T(8,128)(2,1)}, bf16[64,8192]{1,0:T(8,128)(2,1)}, u32[]{:S(2)}, u32[]{:S(2)}) %collective-permute-start.5) | collective-permute-done | bytes 1048608 | tf_op jit(solution)/shard_map/ppermute | solution.py:35
  147.9 1.4 convert_element_type.62
  149.3 21.4 %collective-permute-done.4 = bf16[64,8192]{1,0:T(8,128)(2,1)} collective-permute-done((bf16[64,8192]{1,0:T(8,128)(2,1)}, bf16[64,8192]{1,0:T(8,128)(2,1)}, u32[]{:S(2)}, u32[]{:S(2)}) %collective-permute-start.4) | collective-permute-done | bytes 1048608 | tf_op jit(solution)/shard_map/ppermute | solution.py:35
  170.8 1.4 convert_element_type.60
  172.1 4.0 %fusion.1 = (f32[86,8192]{1,0:T(8,128)}, f32[86,8192]{1,0:T(8,128)}) fusion(s32[]{:T(128)S(6)} %select_n.100, f32[64,8192]{1,0:T(8,128)S(1)} %get-tuple-element.17, f32[64,8192]{1,0:T(8,128)S(1)} %convert_element_type.62, f32[86]{0:T(128)S(1)} %pad_dynamic-slice_fusion.6, f32[64,8192]{1,0:T(8,128)S(1)} %convert_element_type.60, f32[64,8192]{1,0:T(8,128)S(1)} %copy-done.3), kind=kLoop, calls=%fused_computation.10 | loop fusion | flops 2818048 | bytes 14025052 | tf_op jit(solution)/shard_map/concatenate | solution.py:79
  176.1 6.7 %broadcast_in_dim.15 = f32[1,86,8192]{2,0,1:T(1,128)} reshape(f32[86,8192]{1,0:T(8,128)} %get-tuple-element.34) | data formatting | bytes 5636096 | tf_op jit(solution)/shard_map/broadcast_in_dim | solution.py:80
  182.8 4.7 %broadcast_in_dim.16 = f32[1,86,8192]{2,0,1:T(1,128)} reshape(f32[86,8192]{1,0:T(8,128)S(1)} %copy-done.4) | data formatting | bytes 5636096 | tf_op jit(solution)/shard_map/broadcast_in_dim | solution.py:80
  187.5 5.7 %collective-permute-done.3 = bf16[64,8192]{1,0:T(8,128)(2,1)} collective-permute-done((bf16[64,8192]{1,0:T(8,128)(2,1)}, bf16[64,8192]{1,0:T(8,128)(2,1)}, u32[]{:S(2)}, u32[]{:S(2)}) %collective-permute-start.3) | collective-permute-done | bytes 1048608 | tf_op jit(solution)/shard_map/ppermute | solution.py:35
  193.2 3.4 %fusion.10 = bf16[1,86,8192]{2,1,0:T(8,128)(2,1)} fusion(s32[]{:T(128)S(6)} %select_n.100, bf16[64,8192]{1,0:T(8,128)(2,1)} %copy-done.5, bf16[64,8192]{1,0:T(8,128)(2,1)} %collective-permute-done.3, bf16[86]{0:T(256)(128)(2,1)S(1)} %pad_dynamic-slice_fusion.7), kind=kLoop, calls=%fused_computation.23 | loop fusion | flops 4227072 | bytes 3506352 | tf_op jit(solution)/shard_map/broadcast_in_dim | solution.py:80
  196.6 33.4 %all-gather.6.cloned.1.call-done = bf16[8,256,1024]{2,1,0:T(8,128)(2,1)} async-done(((bf16[8,64,1024]{2,1,0:T(8,128)(2,1)}), bf16[8,256,1024]{2,1,0:T(8,128)(2,1)}) %all-gather.6.cloned.1.call-update) | async-done | bytes 4194320 | tf_op jit(solution)/shard_map/all_gather | solution.py:73
  230.0 8.0 %convert_bitcast_fusion = bf16[1024,1024]{0,1:T(8,128)(2,1)S(1)} fusion(bf16[2048,1024]{1,0:T(8,128)(2,1)} %bitcast.88, bf16[1024,2048]{1,0:T(8,128)(2,1)} %all-gather.4.cloned.1.call-done), kind=kOutput, calls=%fused_computation.20 | convolution fusion | flops 4296015872 | bytes 10485760 | tf_op jit(solution)/shard_map/dot_general | solution.py:83
  238.1 2.6 %copy.13 = bf16[1024,1024]{1,0:T(8,128)(2,1)} copy(bf16[1024,1024]{0,1:T(8,128)(2,1)S(1)} %convert_bitcast_fusion) | data formatting | bytes 4194304
  (62 shorter events, 18.4 us)
Async XLA Ops:
  7.2 1.1 copy-start
  7.2 189.4 %all-gather.4.cloned.1.call-start = ((), (), s32[]{:S(2)}) async-start(), calls=%async_computation | async-start | bytes 4718592 | tf_op jit(solution)/shard_map/all_gather | solution.py:45
  7.9 222.1 %all-gather.6.cloned.1.call-start = ((), (), s32[]{:S(2)}) async-start(), calls=%async_computation.1 | async-start | bytes 5242880 | tf_op jit(solution)/shard_map/all_gather | solution.py:73
  24.1 28.1 %collective-permute-start.2 = (bf16[64,8192]{1,0:T(8,128)(2,1)}, bf16[64,8192]{1,0:T(8,128)(2,1)S(1)}, u32[]{:S(2)}, u32[]{:S(2)}) collective-permute-start(bf16[64,8192]{1,0:T(8,128)(2,1)} %get-tuple-element.23), channel_id=1, source_target_pairs={{0,24},{8,16},{16,8},{24,0},{1,25},{9,17},{17,9},{25,1},{2,26},{10... | collective-permute-start | bytes 3145736 | tf_op jit(solution)/shard_map/ppermute | solution.py:25
  27.9 45.8 %collective-permute-start.1 = (bf16[64,8192]{1,0:T(8,128)(2,1)}, bf16[64,8192]{1,0:T(8,128)(2,1)S(1)}, u32[]{:S(2)}, u32[]{:S(2)}) collective-permute-start(bf16[64,8192]{1,0:T(8,128)(2,1)} %get-tuple-element.24), channel_id=1, source_target_pairs={{0,16},{8,24},{16,0},{24,8},{1,17},{9,25},{17,1},{25,9},{2,18},{10... | collective-permute-start | bytes 3145736 | tf_op jit(solution)/shard_map/ppermute | solution.py:25
  28.4 46.3 %collective-permute-start = (bf16[64,8192]{1,0:T(8,128)(2,1)}, bf16[64,8192]{1,0:T(8,128)(2,1)}, u32[]{:S(2)}, u32[]{:S(2)}) collective-permute-start(bf16[64,8192]{1,0:T(8,128)(2,1)} %get-tuple-element.22), channel_id=1, source_target_pairs={{0,8},{8,0},{16,24},{24,16},{1,9},{9,1},{17,25},{25,17},{2,10},{10... | collective-permute-start | bytes 3145736 | tf_op jit(solution)/shard_map/ppermute | solution.py:25
  29.2 51.3 %copy-start.8 = (bf16[1,64,8192]{2,1,0:T(8,128)(2,1)S(1)}, bf16[1,64,8192]{2,1,0:T(8,128)(2,1)}, u32[]{:S(2)}) copy-start(bf16[1,64,8192]{2,1,0:T(8,128)(2,1)} %param.9) | copy-start | bytes 3145732
  52.1 21.6 %copy-start.6 = (bf16[64,8192]{1,0:T(8,128)(2,1)}, bf16[64,8192]{1,0:T(8,128)(2,1)S(1)}, u32[]{:S(2)}) copy-start(bf16[64,8192]{1,0:T(8,128)(2,1)S(1)} %collective-permute-done.2) | copy-start | bytes 3145732
  73.7 1.0 copy-start.7
  80.6 1.3 copy-start.2
  81.9 2.9 %copy-start.5 = (bf16[64,8192]{1,0:T(8,128)(2,1)}, bf16[64,8192]{1,0:T(8,128)(2,1)S(1)}, u32[]{:S(2)}) copy-start(bf16[64,8192]{1,0:T(8,128)(2,1)S(1)} %fusion.7) | copy-start | bytes 3145732
  84.8 8.1 %collective-permute-start.6 = (bf16[64,1024]{1,0:T(8,128)(2,1)S(1)}, bf16[64,1024]{1,0:T(8,128)(2,1)S(1)}, u32[]{:S(2)}, u32[]{:S(2)}) collective-permute-start(bf16[64,1024]{1,0:T(8,128)(2,1)S(1)} %bitcast.87), channel_id=1, source_target_pairs={{0,1},{1,2},{2,3},{3,4},{4,5},{5,6},{6,7},{7,0},{8,9},{9,10},{10,1... | collective-permute-start | bytes 393224 | tf_op jit(solution)/shard_map/ppermute | solution.py:67
  85.0 9.9 %collective-permute-start.7 = (bf16[64,1024]{1,0:T(8,128)(2,1)S(1)}, bf16[64,1024]{1,0:T(8,128)(2,1)S(1)}, u32[]{:S(2)}, u32[]{:S(2)}) collective-permute-start(bf16[64,1024]{1,0:T(8,128)(2,1)S(1)} %bitcast.86), channel_id=1, source_target_pairs={{0,2},{1,3},{2,4},{3,5},{4,6},{5,7},{6,0},{7,1},{8,10},{9,11},{10,... | collective-permute-start | bytes 393224 | tf_op jit(solution)/shard_map/ppermute | solution.py:67
  86.9 16.7 %collective-permute-start.8 = (bf16[64,1024]{1,0:T(8,128)(2,1)S(1)}, bf16[64,1024]{1,0:T(8,128)(2,1)S(1)}, u32[]{:S(2)}, u32[]{:S(2)}) collective-permute-start(bf16[64,1024]{1,0:T(8,128)(2,1)S(1)} %bitcast.85), channel_id=1, source_target_pairs={{0,3},{1,4},{2,5},{3,6},{4,7},{5,0},{6,1},{7,2},{8,11},{9,12},{10,... | collective-permute-start | bytes 393224 | tf_op jit(solution)/shard_map/ppermute | solution.py:67
  89.5 14.8 %collective-permute-start.9 = (bf16[64,1024]{1,0:T(8,128)(2,1)S(1)}, bf16[64,1024]{1,0:T(8,128)(2,1)S(1)}, u32[]{:S(2)}, u32[]{:S(2)}) collective-permute-start(bf16[64,1024]{1,0:T(8,128)(2,1)S(1)} %bitcast.84), channel_id=1, source_target_pairs={{0,4},{1,5},{2,6},{3,7},{4,0},{5,1},{6,2},{7,3},{8,12},{9,13},{10,... | collective-permute-start | bytes 393224 | tf_op jit(solution)/shard_map/ppermute | solution.py:67
  90.8 14.1 %collective-permute-start.10 = (bf16[64,1024]{1,0:T(8,128)(2,1)S(1)}, bf16[64,1024]{1,0:T(8,128)(2,1)S(1)}, u32[]{:S(2)}, u32[]{:S(2)}) collective-permute-start(bf16[64,1024]{1,0:T(8,128)(2,1)S(1)} %bitcast.83), channel_id=1, source_target_pairs={{0,5},{1,6},{2,7},{3,0},{4,1},{5,2},{6,3},{7,4},{8,13},{9,14},{10,... | collective-permute-start | bytes 393224 | tf_op jit(solution)/shard_map/ppermute | solution.py:67
  92.9 12.7 %collective-permute-start.11 = (bf16[64,1024]{1,0:T(8,128)(2,1)S(1)}, bf16[64,1024]{1,0:T(8,128)(2,1)S(1)}, u32[]{:S(2)}, u32[]{:S(2)}) collective-permute-start(bf16[64,1024]{1,0:T(8,128)(2,1)S(1)} %bitcast.82), channel_id=1, source_target_pairs={{0,6},{1,7},{2,0},{3,1},{4,2},{5,3},{6,4},{7,5},{8,14},{9,15},{10,... | collective-permute-start | bytes 393224 | tf_op jit(solution)/shard_map/ppermute | solution.py:67
  95.0 11.3 %collective-permute-start.12 = (bf16[64,1024]{1,0:T(8,128)(2,1)S(1)}, bf16[64,1024]{1,0:T(8,128)(2,1)S(1)}, u32[]{:S(2)}, u32[]{:S(2)}) collective-permute-start(bf16[64,1024]{1,0:T(8,128)(2,1)S(1)} %bitcast.81), channel_id=1, source_target_pairs={{0,7},{1,0},{2,1},{3,2},{4,3},{5,4},{6,5},{7,6},{8,15},{9,8},{10,9... | collective-permute-start | bytes 393224 | tf_op jit(solution)/shard_map/ppermute | solution.py:67
  109.8 38.2 %collective-permute-start.5 = (bf16[64,8192]{1,0:T(8,128)(2,1)}, bf16[64,8192]{1,0:T(8,128)(2,1)}, u32[]{:S(2)}, u32[]{:S(2)}) collective-permute-start(bf16[64,8192]{1,0:T(8,128)(2,1)} %get-tuple-element.16), channel_id=1, source_target_pairs={{8,0},{16,8},{24,16},{9,1},{17,9},{25,17},{10,2},{18,10},{26,18},{... | collective-permute-start | bytes 3145736 | tf_op jit(solution)/shard_map/ppermute | solution.py:35
  111.1 59.7 %collective-permute-start.4 = (bf16[64,8192]{1,0:T(8,128)(2,1)}, bf16[64,8192]{1,0:T(8,128)(2,1)}, u32[]{:S(2)}, u32[]{:S(2)}) collective-permute-start(bf16[64,8192]{1,0:T(8,128)(2,1)} %get-tuple-element.20), channel_id=1, source_target_pairs={{8,0},{16,8},{24,16},{9,1},{17,9},{25,17},{10,2},{18,10},{26,18},{... | collective-permute-start | bytes 3145736 | tf_op jit(solution)/shard_map/ppermute | solution.py:35
  112.6 80.7 %collective-permute-start.3 = (bf16[64,8192]{1,0:T(8,128)(2,1)}, bf16[64,8192]{1,0:T(8,128)(2,1)}, u32[]{:S(2)}, u32[]{:S(2)}) collective-permute-start(bf16[64,8192]{1,0:T(8,128)(2,1)} %copy-done.5), channel_id=1, source_target_pairs={{8,0},{16,8},{24,16},{9,1},{17,9},{25,17},{10,2},{18,10},{26,18},{... | collective-permute-start | bytes 3145736 | tf_op jit(solution)/shard_map/ppermute | solution.py:35
  149.3 22.8 %copy-start.3 = (f32[64,8192]{1,0:T(8,128)S(1)}, f32[64,8192]{1,0:T(8,128)}, u32[]{:S(2)}) copy-start(f32[64,8192]{1,0:T(8,128)} %copy-done.2) | copy-start | bytes 6291460
  176.1 6.7 %copy-start.4 = (f32[86,8192]{1,0:T(8,128)S(1)}, f32[86,8192]{1,0:T(8,128)}, u32[]{:S(2)}) copy-start(f32[86,8192]{1,0:T(8,128)} %get-tuple-element.33) | copy-start | bytes 8454148
  230.0 10.6 %copy-start.1 = (bf16[1024,256]{1,0:T(8,128)(2,1)S(1)}, bf16[1024,256]{1,0:T(8,128)(2,1)}, u32[]{:S(2)}) copy-start(bf16[1024,256]{1,0:T(8,128)(2,1)} %param.7) | copy-start | bytes 1572868
Sparse Core Ops, SparseCore 0:
  9.6 50.4 all-gather.3
  109.9 120.0 all-gather.5
